TPU v7x, 32 devices: a whole 2x2x4 slice. The times are simulated.
32 devices in a mesh: dp: 16 (over z, y, x), mp: 2 (over core).
Axes of the slice: x: 2, y: 2, z: 4, core: 2. Of those that a mesh axis runs over, the one named last changes fastest.
Arguments:
- inputs: bfloat16 [2, 16, 512, 768], P(None, 'dp'), may hold values from -6 to 6
- cotangent: bfloat16 [2, 16, 512, 768], P(None, 'dp'), may hold values from -6 to 6
- lengths: int32 [2, 16], P(None, 'dp'), may hold values from 64 to 256, as said below
- proj_weight: float32 [768, 3, 768], P('dp', None, 'mp'), may hold values from -0.21875 to 0.21875
- output_weight: float32 [768, 768], P('mp', 'dp'), may hold values from -0.875 to 0.875
- upper_weight: float32 [768, 3072], P('dp', 'mp'), may hold values from -0.21875 to 0.21875
- lower_weight: float32 [3072, 768], P('mp', 'dp'), may hold values from -0.109375 to 0.109375
- norm_gains: float32 [2, 768], P(None, 'dp'), may hold values from 0.5 to 1.5
- proj_first: float32 [768, 3, 768], P('dp', None, 'mp'), may hold values from -32 to 32
- output_first: float32 [768, 768], P('mp', 'dp'), may hold values from -7 to 7
- upper_first: float32 [768, 3072], P('dp', 'mp'), may hold values from -20 to 20
- lower_first: float32 [3072, 768], P('mp', 'dp'), may hold values from -40 to 40
- gains_first: float32 [2, 768], P(None, 'dp'), may hold values from -32 to 32
- proj_second: float32 [768, 3, 768], P('dp', None, 'mp'), may hold values from 67.1744 to 1081.344
- output_second: float32 [768, 768], P('mp', 'dp'), may hold values from 2.686976 to 43.08992
- upper_second: float32 [768, 3072], P('dp', 'mp'), may hold values from 24.24832 to 386.6624
- lower_second: float32 [3072, 768], P('mp', 'dp'), may hold values from 96.99328 to 1548.288
- gains_second: float32 [2, 768], P(None, 'dp'), may hold values from 67.1744 to 1081.344
Outputs:
- outputs: bfloat16 [2, 16, 512, 768], P(None, 'dp')
- input_grad: float32 [2, 16, 512, 768], P(None, 'dp')
- proj_new: float32 [768, 3, 768], P('dp', None, 'mp')
- output_new: float32 [768, 768], P('mp', 'dp')
- upper_new: float32 [768, 3072], P('dp', 'mp')
- lower_new: float32 [3072, 768], P('mp', 'dp')
- gains_new: float32 [2, 768], P(None, 'dp')
- proj_first_new: float32 [768, 3, 768], P('dp', None, 'mp')
- output_first_new: float32 [768, 768], P('mp', 'dp')
- upper_first_new: float32 [768, 3072], P('dp', 'mp')
- lower_first_new: float32 [3072, 768], P('mp', 'dp')
- gains_first_new: float32 [2, 768], P(None, 'dp')
- proj_second_new: float32 [768, 3, 768], P('dp', None, 'mp')
- output_second_new: float32 [768, 768], P('mp', 'dp')
- upper_second_new: float32 [768, 3072], P('dp', 'mp')
- lower_second_new: float32 [3072, 768], P('mp', 'dp')
- gains_second_new: float32 [2, 768], P(None, 'dp')
- proj_copy: bfloat16 [768, 3, 768], P('dp', None, 'mp')
- output_copy: bfloat16 [768, 768], P('mp', 'dp')
- upper_copy: bfloat16 [768, 3072], P('dp', 'mp')
- lower_copy: bfloat16 [3072, 768], P('mp', 'dp')
- gains_copy: bfloat16 [2, 768], P(None, 'dp')
Inputs may be any that keep to these rules, and one draw needn't show every extreme that they name: `lengths`: each length is a multiple of 16, and in each micro-batch at least one sequence has exactly 256 positions.
All inputs are finite; a program needn't handle non-finite values.
Results may differ from a plain program's by a relative error of at most 0.015.
The roundings to bfloat16 on the way count: a program that leaves them out, or rounds other values in their place, can miss the bound.
Values may be sent and summed in bfloat16 or wider, within the bound.
No kernel may reach another device: no remote copies, remote signals or barrier semaphores. Data moves between devices by JAX's collectives and lax.ppermute only.
A program may use at most 128 MiB of HBM per device.

v0:
```python
from functools import partial

import jax
import jax.numpy as jnp
from jax import lax
from jax.sharding import PartitionSpec as P

HD = 64
BLOCK = 16
LEN = 256
STEP = 10


EPSILON = 1e-05
BETA_ONE = 0.9
BETA_TWO = 0.95
ADAM_EPS = 1e-08
DECAY = 0.1
RATE_MATRIX = 0.02
RATE_OUTPUT = 0.1
RATE_GAIN = 0.8


def normalize(values):
    centre = jnp.mean(values, axis=-1, keepdims=True)
    shifted = values - centre
    spread = jnp.mean(shifted * shifted, axis=-1, keepdims=True)
    return shifted * lax.rsqrt(spread + EPSILON)


def scaled_norm(values, gain):
    return normalize(values) * gain


def rotation(row_count, head_width):
    halfway = head_width // 2
    freqs = 10000.0 ** (-2.0 * jnp.arange(halfway).astype(jnp.float32) / head_width)
    places = (jnp.arange(row_count) % LEN).astype(jnp.float32)
    angles = places[:, None] * freqs[None, :]
    return (jnp.cos(angles), jnp.sin(angles))


def rotate(vectors, cosine, sine):
    halfway = vectors.shape[-1] // 2
    front = vectors[..., :halfway]
    behind = vectors[..., halfway:]
    cos_cols = cosine[:, None, :]
    sin_cols = sine[:, None, :]
    return jnp.concatenate(
        [front * cos_cols - behind * sin_cols, behind * cos_cols + front * sin_cols], axis=-1
    )


def allowed(query_rows, key_rows, length):
    query_clean = query_rows >= LEN
    key_clean = key_rows >= LEN
    query_place = query_rows - LEN * query_clean.astype(jnp.int32)
    key_place = key_rows - LEN * key_clean.astype(jnp.int32)
    query_block = (query_place // BLOCK)[:, None]
    key_block = (key_place // BLOCK)[None, :]
    noisy_rule = jnp.where(key_clean[None, :], key_block < query_block, key_block == query_block)
    clean_rule = key_clean[None, :] & (key_block <= query_block)
    rule = jnp.where(query_clean[:, None], clean_rule, noisy_rule)
    return (rule & (key_place < length)[None, :]).astype(jnp.int32)


def attend_forward(query_states, key_states, value_states, length):
    row_count = key_states.shape[0]
    block_rows = min(512, row_count)
    score_scale = query_states.shape[-1] ** (-0.5)
    key_rows = jnp.arange(row_count, dtype=jnp.int32)

    def one_block(block_index):
        first_row = block_index * block_rows
        scores = (
            jnp.einsum("qhd,khd->hqk", query_states, key_states, preferred_element_type=jnp.float32)
            * score_scale
        )
        visible = (
            allowed(first_row + jnp.arange(block_rows, dtype=jnp.int32), key_rows, length) == 1
        )
        scores = jnp.where(visible[None], scores, -1e30)
        maximum = jnp.max(scores, axis=-1, keepdims=True)
        raised = jnp.exp(scores - maximum)
        summed = jnp.sum(raised, axis=-1, keepdims=True)
        weights = (raised / summed).astype(jnp.bfloat16)
        result = jnp.einsum(
            "hqk,khd->qhd", weights, value_states, preferred_element_type=jnp.float32
        )
        return (result.astype(jnp.bfloat16), (maximum + jnp.log(summed))[:, :, 0])

    results, logsums = lax.map(one_block, jnp.arange(row_count // block_rows))
    return (results.reshape(query_states.shape), logsums)


def attend_backward(query_states, key_states, value_states, head_grads, logsums, length):
    row_count = key_states.shape[0]
    block_rows = min(512, row_count)
    score_scale = query_states.shape[-1] ** (-0.5)
    key_rows = jnp.arange(row_count, dtype=jnp.int32)

    def one_block(carried, block_index):
        key_grads, value_grads = carried
        first_row = block_index * block_rows
        scores = (
            jnp.einsum("qhd,khd->hqk", query_states, key_states, preferred_element_type=jnp.float32)
            * score_scale
        )
        visible = (
            allowed(first_row + jnp.arange(block_rows, dtype=jnp.int32), key_rows, length) == 1
        )
        scores = jnp.where(visible[None], scores, -1e30)
        softmaxed = jnp.exp(scores - logsums[block_index][:, :, None])
        prob_grads = jnp.einsum(
            "qhd,khd->hqk", head_grads, value_states, preferred_element_type=jnp.float32
        )
        inner_sum = jnp.sum(softmaxed * prob_grads, axis=-1, keepdims=True)
        score_grads = (softmaxed * (prob_grads - inner_sum)).astype(jnp.bfloat16)
        query_grads = (
            jnp.einsum("hqk,khd->qhd", score_grads, key_states, preferred_element_type=jnp.float32)
            * score_scale
        )
        key_grads = (
            key_grads
            + jnp.einsum(
                "hqk,qhd->khd", score_grads, query_states, preferred_element_type=jnp.float32
            )
            * score_scale
        )
        value_grads = value_grads + jnp.einsum(
            "hqk,qhd->khd",
            softmaxed.astype(jnp.bfloat16),
            head_grads,
            preferred_element_type=jnp.float32,
        )
        return ((key_grads, value_grads), query_grads)

    empty_grads = jnp.zeros(key_states.shape, jnp.float32)
    (key_grads, value_grads), query_grads = lax.scan(
        one_block, (empty_grads, empty_grads), jnp.arange(row_count // block_rows)
    )
    return (query_grads.reshape(key_states.shape), key_grads, value_grads)


def adamw_update(weight, first, second, grad, rate, decay):
    first_new = BETA_ONE * first + (1.0 - BETA_ONE) * grad
    second_new = BETA_TWO * second + (1.0 - BETA_TWO) * grad * grad
    corrected = (
        first_new
        / (1.0 - BETA_ONE**STEP)
        / (jnp.sqrt(second_new / (1.0 - BETA_TWO**STEP)) + ADAM_EPS)
    )
    return (weight - rate * (corrected + decay * weight), first_new, second_new)


def shards(
    inputs,
    cotangent,
    lengths,
    proj_weight,
    output_weight,
    upper_weight,
    lower_weight,
    norm_gains,
    proj_first,
    output_first,
    upper_first,
    lower_first,
    gains_first,
    proj_second,
    output_second,
    upper_second,
    lower_second,
    gains_second,
):
    micro_count, seq_count, row_count, width = inputs.shape
    feat_count = proj_weight.shape[2]
    head_count = feat_count // HD
    gelu_exact = partial(jax.nn.gelu, approximate=False)
    cosine, sine = rotation(row_count, HD)
    places = jnp.arange(row_count, dtype=jnp.int32) % LEN
    results_list = []
    grads_list = []
    reduced = None
    for micro_index in range(micro_count):
        micro_in = inputs[micro_index]
        micro_len = lengths[micro_index]
        proj_c = lax.all_gather(proj_weight.astype(jnp.bfloat16), "dp", axis=0, tiled=True)
        output_c = lax.all_gather(output_weight.astype(jnp.bfloat16), "dp", axis=1, tiled=True)
        upper_c = lax.all_gather(upper_weight.astype(jnp.bfloat16), "dp", axis=0, tiled=True)
        lower_c = lax.all_gather(lower_weight.astype(jnp.bfloat16), "dp", axis=1, tiled=True)
        gains_c = lax.all_gather(norm_gains.astype(jnp.bfloat16), "dp", axis=1, tiled=True)
        gain_one = gains_c[0].astype(jnp.float32)
        gain_two = gains_c[1].astype(jnp.float32)
        flat_in = micro_in.astype(jnp.float32).reshape(-1, width)
        first_norm = scaled_norm(flat_in, gain_one).astype(jnp.bfloat16)
        mixed = jnp.einsum("rd,dcf->rcf", first_norm, proj_c, preferred_element_type=jnp.float32)
        mixed = mixed.reshape(seq_count, row_count, 3, head_count, HD)
        query_states = rotate(mixed[:, :, 0], cosine, sine).astype(jnp.bfloat16)
        key_states = rotate(mixed[:, :, 1], cosine, sine).astype(jnp.bfloat16)
        value_states = mixed[:, :, 2].astype(jnp.bfloat16)
        heads_out, logsums = lax.map(
            lambda packed: attend_forward(*packed),
            (query_states, key_states, value_states, micro_len),
        )
        flat_heads = heads_out.reshape(-1, feat_count)
        attn_part = jnp.dot(flat_heads, output_c, preferred_element_type=jnp.float32)
        middle = flat_in + lax.psum(attn_part.astype(jnp.bfloat16), "mp").astype(jnp.float32)
        second_norm = scaled_norm(middle, gain_two).astype(jnp.bfloat16)
        upper = jnp.dot(second_norm, upper_c, preferred_element_type=jnp.float32)
        active = gelu_exact(upper).astype(jnp.bfloat16)
        ffn_part = jnp.dot(active, lower_c, preferred_element_type=jnp.float32)
        result = middle + lax.psum(ffn_part.astype(jnp.bfloat16), "mp").astype(jnp.float32)
        valid = (places[None, :] < micro_len[:, None]).astype(jnp.float32)
        up_grad = (cotangent[micro_index].astype(jnp.float32) * valid[:, :, None]).reshape(
            -1, width
        )
        up_low = up_grad.astype(jnp.bfloat16)
        lower_grad = jnp.einsum("rf,rd->fd", active, up_low, preferred_element_type=jnp.float32)
        active_grad = jnp.einsum("rd,fd->rf", up_low, lower_c, preferred_element_type=jnp.float32)
        upper_grad = jax.vjp(gelu_exact, upper)[1](active_grad)[0].astype(jnp.bfloat16)
        upper_wgrad = jnp.einsum(
            "rd,rf->df", second_norm, upper_grad, preferred_element_type=jnp.float32
        )
        second_back = lax.psum(
            jnp.einsum("rf,df->rd", upper_grad, upper_c, preferred_element_type=jnp.float32).astype(
                jnp.bfloat16
            ),
            "mp",
        ).astype(jnp.float32)
        middle_part, gain_two_grad = jax.vjp(scaled_norm, middle, gain_two)[1](second_back)
        middle_grad = up_grad + middle_part
        attn_low = middle_grad.astype(jnp.bfloat16)
        output_grad = jnp.einsum(
            "rf,rd->fd", flat_heads, attn_low, preferred_element_type=jnp.float32
        )
        head_grads = jnp.einsum(
            "rd,fd->rf", attn_low, output_c, preferred_element_type=jnp.float32
        ).astype(jnp.bfloat16)
        head_grads = head_grads.reshape(seq_count, row_count, head_count, HD)
        query_grads, key_grads, value_grads = lax.map(
            lambda packed: attend_backward(*packed),
            (query_states, key_states, value_states, head_grads, logsums, micro_len),
        )
        mixed_grad = jnp.stack(
            [rotate(query_grads, cosine, -sine), rotate(key_grads, cosine, -sine), value_grads],
            axis=2,
        )
        mixed_grad = mixed_grad.astype(jnp.bfloat16).reshape(-1, 3, feat_count)
        proj_grad = jnp.einsum(
            "rd,rcf->dcf", first_norm, mixed_grad, preferred_element_type=jnp.float32
        )
        first_back = lax.psum(
            jnp.einsum(
                "rcf,dcf->rd", mixed_grad, proj_c, preferred_element_type=jnp.float32
            ).astype(jnp.bfloat16),
            "mp",
        ).astype(jnp.float32)
        input_part, gain_one_grad = jax.vjp(scaled_norm, flat_in, gain_one)[1](first_back)
        input_grad = middle_grad + input_part
        grads = (
            proj_grad,
            output_grad,
            upper_wgrad,
            lower_grad,
            jnp.stack([gain_one_grad, gain_two_grad]),
        )
        result, input_grad, grads = (
            result.astype(jnp.bfloat16).reshape(micro_in.shape),
            input_grad.reshape(micro_in.shape),
            grads,
        )
        results_list.append(result)
        grads_list.append(input_grad)
        summed_part = (
            lax.psum_scatter(grads[0], "dp", scatter_dimension=0, tiled=True),
            lax.psum_scatter(grads[1], "dp", scatter_dimension=1, tiled=True),
            lax.psum_scatter(grads[2], "dp", scatter_dimension=0, tiled=True),
            lax.psum_scatter(grads[3], "dp", scatter_dimension=1, tiled=True),
            lax.psum_scatter(grads[4], "dp", scatter_dimension=1, tiled=True),
        )
        reduced = summed_part if micro_index == 0 else jax.tree.map(jnp.add, reduced, summed_part)
    proj_new, proj_first_new, proj_second_new = adamw_update(
        proj_weight, proj_first, proj_second, reduced[0], RATE_MATRIX, DECAY
    )
    output_new, output_first_new, output_second_new = adamw_update(
        output_weight, output_first, output_second, reduced[1], RATE_OUTPUT, DECAY
    )
    upper_new, upper_first_new, upper_second_new = adamw_update(
        upper_weight, upper_first, upper_second, reduced[2], RATE_MATRIX, DECAY
    )
    lower_new, lower_first_new, lower_second_new = adamw_update(
        lower_weight, lower_first, lower_second, reduced[3], RATE_MATRIX, DECAY
    )
    gains_new, gains_first_new, gains_second_new = adamw_update(
        norm_gains, gains_first, gains_second, reduced[4], RATE_GAIN, 0.0
    )
    return (
        jnp.stack(results_list),
        jnp.stack(grads_list),
        proj_new,
        output_new,
        upper_new,
        lower_new,
        gains_new,
        proj_first_new,
        output_first_new,
        upper_first_new,
        lower_first_new,
        gains_first_new,
        proj_second_new,
        output_second_new,
        upper_second_new,
        lower_second_new,
        gains_second_new,
        proj_new.astype(jnp.bfloat16),
        output_new.astype(jnp.bfloat16),
        upper_new.astype(jnp.bfloat16),
        lower_new.astype(jnp.bfloat16),
        gains_new.astype(jnp.bfloat16),
    )


def solution(mesh):
    in_specs = (
        P(None, "dp", None, None),
        P(None, "dp", None, None),
        P(None, "dp"),
        P("dp", None, "mp"),
        P("mp", "dp"),
        P("dp", "mp"),
        P("mp", "dp"),
        P(None, "dp"),
        P("dp", None, "mp"),
        P("mp", "dp"),
        P("dp", "mp"),
        P("mp", "dp"),
        P(None, "dp"),
        P("dp", None, "mp"),
        P("mp", "dp"),
        P("dp", "mp"),
        P("mp", "dp"),
        P(None, "dp"),
    )
    out_specs = (
        P(None, "dp", None, None),
        P(None, "dp", None, None),
        P("dp", None, "mp"),
        P("mp", "dp"),
        P("dp", "mp"),
        P("mp", "dp"),
        P(None, "dp"),
        P("dp", None, "mp"),
        P("mp", "dp"),
        P("dp", "mp"),
        P("mp", "dp"),
        P(None, "dp"),
        P("dp", None, "mp"),
        P("mp", "dp"),
        P("dp", "mp"),
        P("mp", "dp"),
        P(None, "dp"),
        P("dp", None, "mp"),
        P("mp", "dp"),
        P("dp", "mp"),
        P("mp", "dp"),
        P(None, "dp"),
    )
    return jax.shard_map(shards, mesh=mesh, in_specs=in_specs, out_specs=out_specs, check_vma=False)
```

profile of v0, /device:TPU:0, one launch (start us, length us, event | category | flops | bytes accessed | tf_op | source)
XLA Modules:
  0.0 1132.2 jit_solution(2452046749701401880)
XLA Ops:
  9.7 42.2 %all-gather = bf16[16,48,2]{1,2,0:T(2,128)(2,1)S(1)} all-gather(bf16[1,48,2]{1,2,0:T(2,128)(2,1)S(1)} %convert_bitcast_fusion.4), channel_id=1, replica_groups=mesh['dp'=16,'mp'=2] {'dp'}, dimensions={0}, use_global_device_ids=true | all-gather | bytes 3264 | tf_op jit(solution)/shard_map/all_gather | solution.py:192
  59.6 39.6 %all_gather.22 = bf16[384,768]{0,1:T(8,128)(2,1)S(1)} all-gather(bf16[384,48]{0,1:T(8,128)(2,1)S(1)} %convert_element_type.556), channel_id=1, replica_groups=mesh['dp'=16,'mp'=2] {'dp'}, dimensions={1}, use_global_device_ids=true | all-gather | bytes 626688 | tf_op jit(solution)/shard_map/all_gather | solution.py:189
  99.1 4.0 copy.76
  114.4 16.9 %all-reduce.7.cloned.1.call-done = bf16[512,768]{1,0:T(8,128)(2,1)} async-done(((bf16[512,768]{1,0:T(8,128)(2,1)}), bf16[512,768]{1,0:T(8,128)(2,1)}) %all-reduce.7.cloned.1.call-update) | async-done | bytes 786448 | tf_op jit(solution)/shard_map/psum | solution.py:208
  144.6 18.2 %all-reduce.9.cloned.1.call-done = bf16[512,768]{1,0:T(8,128)(2,1)} async-done(((bf16[512,768]{1,0:T(8,128)(2,1)}), bf16[512,768]{1,0:T(8,128)(2,1)}) %all-reduce.9.cloned.1.call-update) | async-done | bytes 786448 | tf_op jit(solution)/shard_map/psum | solution.py:208
  165.3 64.3 %all-gather.7.cloned.1.call-done = bf16[768,1536]{1,0:T(8,128)(2,1)} async-done(((bf16[48,1536]{1,0:T(8,128)(2,1)}), bf16[768,1536]{1,0:T(8,128)(2,1)}) %all-gather.7.cloned.1.call-update) | async-done | bytes 2359312 | tf_op jit(solution)/shard_map/all_gather | solution.py:190
  229.6 11.0 multiply_convert_fusion.3
  243.5 9.3 multiply_convert_fusion.2
  257.8 136.7 %reduce-scatter.14.cloned.1.call-done = f32[1536,48]{0,1:T(8,128)} async-done(((f32[1536,768]{0,1:T(8,128)}), f32[1536,48]{0,1:T(8,128)}) %reduce-scatter.14.cloned.1.call-update) | async-done | bytes 294928 | tf_op jit(solution)/shard_map/reduce_scatter | solution.py:279
  397.0 62.5 %all-gather.9.cloned.1.call-done = bf16[1536,768]{0,1:T(8,128)(2,1)} async-done(((bf16[1536,48]{0,1:T(8,128)(2,1)}), bf16[1536,768]{0,1:T(8,128)(2,1)}) %all-gather.9.cloned.1.call-update) | async-done | bytes 2359312 | tf_op jit(solution)/shard_map/all_gather | solution.py:191
  459.5 6.0 add_convert_fusion.1
  476.2 4.6 convolution_convert_fusion.2
  483.1 12.4 %all-reduce.13.cloned.1.call-done = (bf16[512,768]{1,0:T(8,128)(2,1)}, bf16[512,768]{1,0:T(8,128)(2,1)}) async-done(((bf16[512,768]{1,0:T(8,128)(2,1)}, bf16[512,768]{1,0:T(8,128)(2,1)}), (bf16[512,768]{1,0:T(8,128)(2,1)}, bf16[512,768]{1,0:T(8,128)(2,1)})) %all-reduce.13.cloned.1.call-update) | async-done | bytes 1572880 | tf_op jit(solution)/shard_map/psum | solution.py:225
  506.7 5.1 multiply_reduce_fusion
  511.8 4.8 multiply_convert_fusion
  521.8 5.1 multiply_reduce_fusion.1
  526.9 4.6 multiply_convert_fusion.1
  566.6 4.4 fusion.97
  571.0 14.6 %all-reduce.11.cloned.1.call-done = (bf16[512,768]{1,0:T(8,128)(2,1)}, bf16[512,768]{1,0:T(8,128)(2,1)}, bf16[512,768]{1,0:T(8,128)(2,1)}, bf16[512,768]{1,0:T(8,128)(2,1)}) async-done(((bf16[512,768]{1,0:T(8,128)(2,1)}, bf16[512,768]{1,0:T(8,128)(2,1)}, bf16[512,768]{1,0:T(8,128)(2,1)}, bf16[512,768]{1,0:T(8,128)(2,1)}), (bf16[512,768]{1,0:T(8,128)(2,1)}, bf16[512,768]{1,0:T(8,128)(2,1)}, ...) | async-done | bytes 3145744 | tf_op jit(solution)/shard_map/psum | solution.py:213
  593.0 5.4 convolution_add_fusion.2
  606.2 110.5 %reduce-scatter.10.cloned.1.call-done = f32[384,48]{0,1:T(8,128)} async-done(((f32[384,768]{0,1:T(8,128)}), f32[384,48]{0,1:T(8,128)}) %reduce-scatter.10.cloned.1.call-update) | async-done | bytes 73744 | tf_op jit(solution)/shard_map/reduce_scatter | solution.py:277
  727.0 115.5 %reduce-scatter.16.cloned.1.call-done = f32[48,2]{1,0:T(8,128)} async-done(((f32[768,2]{1,0:T(8,128)}), f32[48,2]{1,0:T(8,128)}) %reduce-scatter.16.cloned.1.call-update) | async-done | bytes 400
  843.9 137.3 %reduce-scatter.8.cloned.1.call-done = f32[48,3,384]{2,0,1:T(8,128)} async-done(((f32[768,3,384]{2,0,1:T(8,128)}), f32[48,3,384]{2,0,1:T(8,128)}) %reduce-scatter.8.cloned.1.call-update) | async-done | bytes 221200 | tf_op jit(solution)/shard_map/reduce_scatter | solution.py:276
  983.1 139.9 %reduce-scatter.12.cloned.1.call-done = f32[48,1536]{1,0:T(8,128)} async-done(((f32[768,1536]{1,0:T(8,128)}), f32[48,1536]{1,0:T(8,128)}) %reduce-scatter.12.cloned.1.call-update) | async-done | bytes 294928 | tf_op jit(solution)/shard_map/reduce_scatter | solution.py:278
  (384 shorter events, 141.1 us)
Async XLA Ops:
  7.2 91.9 %all-gather.5.cloned.1.call-start = ((), (), s32[]{:S(2)}) async-start(), calls=%async_computation.5 | async-start | bytes 1880064 | tf_op jit(solution)/shard_map/all_gather | solution.py:188
  9.0 122.3 %all-reduce.7.cloned.1.call-start = ((), (), s32[]{:S(2)}) async-start(), calls=%async_computation.6 | async-start | bytes 1572864 | tf_op jit(solution)/shard_map/psum | solution.py:208
  55.6 443.5 %copy-start.65 = (f32[768]{0:T(1024)}, f32[768]{0:T(1024)S(1)}, u32[]{:S(2)}) copy-start(f32[768]{0:T(1024)S(1)} %get-tuple-element.296) | copy-start | bytes 9220
  113.8 49.1 %all-reduce.9.cloned.1.call-start = ((), (), s32[]{:S(2)}) async-start(), calls=%async_computation.9 | async-start | bytes 1572864 | tf_op jit(solution)/shard_map/psum | solution.py:208
  142.3 87.3 %all-gather.7.cloned.1.call-start = ((), (), s32[]{:S(2)}) async-start(), calls=%async_computation.7 | async-start | bytes 2506752 | tf_op jit(solution)/shard_map/all_gather | solution.py:190
  143.1 251.4 %reduce-scatter.14.cloned.1.call-start = ((), (), s32[]{:S(2)}) async-start(), calls=%async_computation.13 | async-start | bytes 5013504 | tf_op jit(solution)/shard_map/reduce_scatter | solution.py:279
  144.6 356.7 %copy-start.81 = (f32[512]{0:T(512)}, f32[512]{0:T(512)S(1)}, u32[]{:S(2)}) copy-start(f32[512]{0:T(512)S(1)} %get-tuple-element.390) | copy-start | bytes 6148
  144.6 356.7 %copy-start.85 = (f32[512]{0:T(512)}, f32[512]{0:T(512)S(1)}, u32[]{:S(2)}) copy-start(f32[512]{0:T(512)S(1)} %get-tuple-element.389) | copy-start | bytes 6148
  144.6 354.5 %copy-start.83 = (f32[512]{0:T(512)}, f32[512]{0:T(512)S(1)}, u32[]{:S(2)}) copy-start(f32[512]{0:T(512)S(1)} %broadcast_multiply_fusion.2) | copy-start | bytes 6148
  164.7 334.4 %copy-start.73 = (f32[512]{0:T(512)}, f32[512]{0:T(512)S(1)}, u32[]{:S(2)}) copy-start(f32[512]{0:T(512)S(1)} %broadcast_multiply_fusion) | copy-start | bytes 6148
  165.3 333.9 %copy-start.89 = (f32[512]{0:T(512)}, f32[512]{0:T(512)S(1)}, u32[]{:S(2)}) copy-start(f32[512]{0:T(512)S(1)} %fusion.159) | copy-start | bytes 6148
  165.3 333.9 %copy-start.77 = (f32[512]{0:T(512)}, f32[512]{0:T(512)S(1)}, u32[]{:S(2)}) copy-start(f32[512]{0:T(512)S(1)} %fusion.161) | copy-start | bytes 6148
  257.7 201.8 %all-gather.9.cloned.1.call-start = ((), (), s32[]{:S(2)}) async-start(), calls=%async_computation.8 | async-start | bytes 2506752 | tf_op jit(solution)/shard_map/all_gather | solution.py:191
  396.8 98.8 %all-reduce.13.cloned.1.call-start = ((), (), s32[]{:S(2)}) async-start(), calls=%async_computation.16 | async-start | bytes 3145728 | tf_op jit(solution)/shard_map/psum | solution.py:225
  476.1 109.5 %all-reduce.11.cloned.1.call-start = ((), (), s32[]{:S(2)}) async-start(), calls=%async_computation.15 | async-start | bytes 6291456 | tf_op jit(solution)/shard_map/psum | solution.py:213
  560.9 155.8 %reduce-scatter.10.cloned.1.call-start = ((), (), s32[]{:S(2)}) async-start(), calls=%async_computation.11 | async-start | bytes 1253376 | tf_op jit(solution)/shard_map/reduce_scatter | solution.py:277
  564.7 277.8 %reduce-scatter.16.cloned.1.call-start = ((), (), s32[]{:S(2)}) async-start(), calls=%async_computation.14 | async-start | bytes 417792
  592.9 388.3 %reduce-scatter.8.cloned.1.call-start = ((), (), s32[]{:S(2)}) async-start(), calls=%async_computation.10 | async-start | bytes 3760128 | tf_op jit(solution)/shard_map/reduce_scatter | solution.py:276
  598.5 524.6 %reduce-scatter.12.cloned.1.call-start = ((), (), s32[]{:S(2)}) async-start(), calls=%async_computation.12 | async-start | bytes 5013504 | tf_op jit(solution)/shard_map/reduce_scatter | solution.py:278
  725.0 256.2 %copy-start.38 = (f32[48,3,384]{2,0,1:T(8,128)S(1)}, f32[48,3,384]{2,0,1:T(8,128)}, u32[]{:S(2)}) copy-start(f32[48,3,384]{2,0,1:T(8,128)} %param.21) | copy-start | bytes 663556
  725.1 256.2 %copy-start.63 = (f32[48,3,384]{2,0,1:T(8,128)S(1)}, f32[48,3,384]{2,0,1:T(8,128)}, u32[]{:S(2)}) copy-start(f32[48,3,384]{2,0,1:T(8,128)} %param.26) | copy-start | bytes 663556
  725.1 398.0 %copy-start.36 = (f32[48,1536]{1,0:T(8,128)S(1)}, f32[48,1536]{1,0:T(8,128)}, u32[]{:S(2)}) copy-start(f32[48,1536]{1,0:T(8,128)} %param.23) | copy-start | bytes 884740
  725.1 397.9 %copy-start.59 = (f32[48,1536]{1,0:T(8,128)S(1)}, f32[48,1536]{1,0:T(8,128)}, u32[]{:S(2)}) copy-start(f32[48,1536]{1,0:T(8,128)} %param.28) | copy-start | bytes 884740
  725.1 397.9 %copy-start.60 = (f32[48,1536]{1,0:T(8,128)S(1)}, f32[48,1536]{1,0:T(8,128)}, u32[]{:S(2)}) copy-start(f32[48,1536]{1,0:T(8,128)} %param.33) | copy-start | bytes 884740
  (114 other events, 2383.4 us)
Sparse Core Ops, SparseCore 0:
  11.3 62.6 all-gather.4
  113.9 17.2 all-reduce.6
  142.4 20.3 all-reduce.8
  166.1 63.4 all-gather.6
  257.9 136.5 reduce-scatter.13
  398.1 61.4 all-gather.8
  476.2 19.3 all-reduce.12
  561.0 24.5 all-reduce.10
  591.1 125.5 reduce-scatter.9
  721.9 120.5 reduce-scatter.15
  847.6 133.5 reduce-scatter.7
  986.2 136.7 reduce-scatter.11
where the time goes:
time: 1140 us; the launch traced here: 1130 us
  waiting for transfers between devices  829 us (73%)
  matrix products  105 us (9%)
  blocking collectives  81.8 us (7%)
  other arithmetic  64.2 us (6%)
  local copies, waits for them, and re-layouts  34.6 us (3%)
  between operations  16 us (1%)
    reduce_scatter x1, waiting for transfers between devices, shards(): lax.psum_scatter(grads[2], 'dp', scatter_dimension=0, tiled=True)  140 us
    reduce_scatter x1, waiting for transfers between devices, shards(): lax.psum_scatter(grads[0], 'dp', scatter_dimension=0, tiled=True)  137 us
    reduce_scatter x1, waiting for transfers between devices, shards(): lax.psum_scatter(grads[3], 'dp', scatter_dimension=1, tiled=True)  137 us
    unnamed x13, waiting for transfers between devices  116 us
    reduce_scatter x1, waiting for transfers between devices, shards(): lax.psum_scatter(grads[1], 'dp', scatter_dimension=1, tiled=True)  111 us
    all_gather x1, waiting for transfers between devices, shards(): lax.all_gather(upper_weight.astype(jnp.bfloat16), 'dp', axis=0, tiled=True)  64.3 us
    all_gather x1, waiting for transfers between devices, shards(): lax.all_gather(lower_weight.astype(jnp.bfloat16), 'dp', axis=1, tiled=True)  62.5 us
    all_gather x1, blocking collectives, shards(): lax.all_gather(norm_gains.astype(jnp.bfloat16), 'dp', axis=1, tiled=True)  42.2 us
  transfers between devices with their start and end apart: 12, of which 11 were waited for; matrix products, arithmetic and copies ran while one was open for 5% of the time, Pallas kernels for 0%

commit v1 on v0

v1 whole, which is shorter than its diff:
```python
from functools import partial

import jax
import jax.numpy as jnp
from jax import lax
from jax.sharding import PartitionSpec as P

HD = 64
BLOCK = 16
LEN = 256
STEP = 10

EPSILON = 1e-05
BETA_ONE = 0.9
BETA_TWO = 0.95
ADAM_EPS = 1e-08
DECAY = 0.1
RATE_MATRIX = 0.02
RATE_OUTPUT = 0.1
RATE_GAIN = 0.8

LANES = 128
BF = jnp.bfloat16
F32 = jnp.float32

NZ, NY, NX = 4, 2, 2
CHIPS = NZ * NY * NX


def chip_pairs(move):
    pairs = []
    for chip in range(CHIPS):
        z, y, x = chip // 4, chip // 2 % 2, chip % 2
        to_z, to_y, to_x = move(z, y, x)
        pairs.append((chip, to_z * 4 + to_y * 2 + to_x))
    return pairs


SWAP_X = chip_pairs(lambda z, y, x: (z, y, 1 - x))
SWAP_Y = chip_pairs(lambda z, y, x: (z, 1 - y, x))
SHIFT_Z = {k: chip_pairs(lambda z, y, x, k=k: ((z + k) % NZ, y, x)) for k in (1, 2, 3)}


def chip_place():
    chip = lax.axis_index("dp")
    return chip // 4, chip // 2 % 2, chip % 2


def exchange(value, pairs):
    return lax.ppermute(value, "dp", pairs)


def gather_rows(shard, cut):
    if lax.axis_size("dp") != CHIPS:
        return lax.all_gather(shard, "dp", axis=0, tiled=True)
    z, y, x = chip_place()
    arrived = [shard] + [exchange(shard, SHIFT_Z[k]) for k in (1, 2, 3)]
    pieces = jnp.stack(arrived)
    order = (z - jnp.arange(NZ)) % NZ

    def one_part(part, first, second, first_bit, second_bit):
        near = exchange(part, first)
        pair = jnp.where(first_bit == 0, jnp.stack([part, near]), jnp.stack([near, part]))
        far = exchange(pair, second)
        return jnp.where(second_bit == 0, jnp.stack([pair, far]), jnp.stack([far, pair]))

    part_a = one_part(pieces[:, :, :cut], SWAP_X, SWAP_Y, x, y)
    part_b = one_part(pieces[:, :, cut:], SWAP_Y, SWAP_X, y, x)
    part_b = part_b.transpose(1, 0, 2, 3, 4)
    whole = jnp.concatenate([part_a, part_b], axis=-1)
    whole = jnp.take(whole, order, axis=2).transpose(2, 0, 1, 3, 4)
    return whole.reshape(CHIPS * shard.shape[0], shard.shape[1])


def scatter_rows(partial_sum, cut):
    size = lax.axis_size("dp")
    if size != CHIPS:
        return lax.psum_scatter(
            partial_sum.astype(BF), "dp", scatter_dimension=0, tiled=True
        ).astype(F32)
    z, y, x = chip_place()
    rows = partial_sum.shape[0] // CHIPS
    grid = partial_sum.reshape(NZ, NY, NX, rows, -1)
    pick = lax.dynamic_index_in_dim

    def one_part(part, first, second, first_axis, first_bit, second_bit):
        sent = pick(part, 1 - first_bit, first_axis, keepdims=False).astype(BF)
        kept = pick(part, first_bit, first_axis, keepdims=False)
        half = kept + exchange(sent, first).astype(F32)
        sent = pick(half, 1 - second_bit, 1, keepdims=False).astype(BF)
        kept = pick(half, second_bit, 1, keepdims=False)
        return kept + exchange(sent, second).astype(F32)

    part_a = one_part(grid[..., :cut], SWAP_X, SWAP_Y, 2, x, y)
    part_b = one_part(grid[..., cut:], SWAP_Y, SWAP_X, 1, y, x)
    column = jnp.concatenate([part_a, part_b], axis=-1)
    total = pick(column, z, 0, keepdims=False)
    for k in (1, 2, 3):
        sent = pick(column, (z + k) % NZ, 0, keepdims=False).astype(BF)
        total = total + exchange(sent, SHIFT_Z[k]).astype(F32)
    return total


def sum_pair(value):
    other = lax.ppermute(value, "mp", [(0, 1), (1, 0)])
    return value.astype(F32) + other.astype(F32)


def normalize(values):
    centre = jnp.mean(values, axis=-1, keepdims=True)
    shifted = values - centre
    spread = jnp.mean(shifted * shifted, axis=-1, keepdims=True)
    return shifted * lax.rsqrt(spread + EPSILON)


def scaled_norm(values, gain):
    return normalize(values) * gain


def rotation(row_count, head_width):
    halfway = head_width // 2
    freqs = 10000.0 ** (-2.0 * jnp.arange(halfway).astype(jnp.float32) / head_width)
    places = (jnp.arange(row_count) % LEN).astype(jnp.float32)
    angles = places[:, None] * freqs[None, :]
    return (jnp.cos(angles), jnp.sin(angles))


def rotate(vectors, cosine, sine):
    halfway = vectors.shape[-1] // 2
    front = vectors[..., :halfway]
    behind = vectors[..., halfway:]
    cos_cols = cosine[:, None, :]
    sin_cols = sine[:, None, :]
    return jnp.concatenate(
        [front * cos_cols - behind * sin_cols, behind * cos_cols + front * sin_cols], axis=-1
    )


def allowed(query_rows, key_rows, length):
    query_clean = query_rows >= LEN
    key_clean = key_rows >= LEN
    query_place = query_rows - LEN * query_clean.astype(jnp.int32)
    key_place = key_rows - LEN * key_clean.astype(jnp.int32)
    query_block = (query_place // BLOCK)[:, None]
    key_block = (key_place // BLOCK)[None, :]
    noisy_rule = jnp.where(key_clean[None, :], key_block < query_block, key_block == query_block)
    clean_rule = key_clean[None, :] & (key_block <= query_block)
    rule = jnp.where(query_clean[:, None], clean_rule, noisy_rule)
    return rule & (key_place < length)[None, :]


def attend_scores(query, key, length):
    rows = jnp.arange(query.shape[1], dtype=jnp.int32)
    scores = jnp.einsum("hqd,hkd->hqk", query, key, preferred_element_type=F32) * (HD**-0.5)
    return jnp.where(allowed(rows, rows, length)[None], scores, -1e30)


def attend_forward(query, key, value, length):
    scores = attend_scores(query, key, length)
    maximum = jnp.max(scores, axis=-1, keepdims=True)
    raised = jnp.exp(scores - maximum)
    summed = jnp.sum(raised, axis=-1, keepdims=True)
    weights = (raised / summed).astype(BF)
    result = jnp.einsum("hqk,hkd->qhd", weights, value, preferred_element_type=F32)
    return result.astype(BF), maximum + jnp.log(summed)


def attend_backward(query, key, value, head_grads, logsums, length):
    scores = attend_scores(query, key, length)
    softmaxed = jnp.exp(scores - logsums)
    prob_grads = jnp.einsum("qhd,hkd->hqk", head_grads, value, preferred_element_type=F32)
    inner_sum = jnp.sum(softmaxed * prob_grads, axis=-1, keepdims=True)
    score_grads = (softmaxed * (prob_grads - inner_sum)).astype(BF)
    scale = HD**-0.5
    query_grads = jnp.einsum("hqk,hkd->qhd", score_grads, key, preferred_element_type=F32) * scale
    key_grads = jnp.einsum("hqk,hqd->khd", score_grads, query, preferred_element_type=F32) * scale
    value_grads = jnp.einsum(
        "hqk,qhd->khd", softmaxed.astype(BF), head_grads, preferred_element_type=F32
    )
    return query_grads, key_grads, value_grads


def adamw_update(weight, first, second, grad, rate, decay):
    first_new = BETA_ONE * first + (1.0 - BETA_ONE) * grad
    second_new = BETA_TWO * second + (1.0 - BETA_TWO) * grad * grad
    corrected = (
        first_new
        / (1.0 - BETA_ONE**STEP)
        / (jnp.sqrt(second_new / (1.0 - BETA_TWO**STEP)) + ADAM_EPS)
    )
    return (weight - rate * (corrected + decay * weight), first_new, second_new)


def shards(
    inputs,
    cotangent,
    lengths,
    proj_weight,
    output_weight,
    upper_weight,
    lower_weight,
    norm_gains,
    proj_first,
    output_first,
    upper_first,
    lower_first,
    gains_first,
    proj_second,
    output_second,
    upper_second,
    lower_second,
    gains_second,
):
    micro_count, seq_count, row_count, width = inputs.shape
    feat_count = proj_weight.shape[2]
    head_count = feat_count // HD
    hidden = upper_weight.shape[1]
    shard_rows = proj_weight.shape[0]
    gelu_exact = partial(jax.nn.gelu, approximate=False)
    cosine, sine = rotation(row_count, HD)
    places = jnp.arange(row_count, dtype=jnp.int32) % LEN

    gain_columns = jnp.pad(norm_gains.T.astype(BF), ((0, 0), (0, LANES - 2)))
    proj_cols = 3 * feat_count
    shard_one = jnp.concatenate(
        [
            gain_columns,
            proj_weight.astype(BF).reshape(shard_rows, proj_cols),
            output_weight.astype(BF).T,
        ],
        axis=1,
    )
    cut = LANES + (proj_cols + feat_count) // 2
    whole_one = gather_rows(shard_one, cut)
    gains_c = whole_one[:, :2].T.astype(F32)
    proj_c = whole_one[:, LANES : LANES + proj_cols]
    output_t = whole_one[:, LANES + proj_cols :]
    upper_c = gather_rows(upper_weight.astype(BF), hidden // 2)
    lower_t = gather_rows(lower_weight.astype(BF).T, hidden // 2)
    gain_one, gain_two = gains_c[0], gains_c[1]

    results_list, kept = [], []
    for micro in range(micro_count):
        length = lengths[micro, 0]
        flat_in = inputs[micro].astype(F32).reshape(-1, width)
        first_norm = scaled_norm(flat_in, gain_one).astype(BF)
        mixed = jnp.dot(first_norm, proj_c, preferred_element_type=F32)
        mixed = mixed.reshape(row_count, 3, head_count, HD)
        query = rotate(mixed[:, 0], cosine, sine).astype(BF).transpose(1, 0, 2)
        key = rotate(mixed[:, 1], cosine, sine).astype(BF).transpose(1, 0, 2)
        value = mixed[:, 2].astype(BF).transpose(1, 0, 2)
        heads_out, logsums = attend_forward(query, key, value, length)
        flat_heads = heads_out.reshape(-1, feat_count)
        attn_part = jnp.einsum("rf,df->rd", flat_heads, output_t, preferred_element_type=F32)
        middle = flat_in + sum_pair(attn_part.astype(BF))
        second_norm = scaled_norm(middle, gain_two).astype(BF)
        upper = jnp.dot(second_norm, upper_c, preferred_element_type=F32)
        active = gelu_exact(upper).astype(BF)
        valid = (places < length).astype(F32)
        up_grad = cotangent[micro, 0].astype(F32) * valid[:, None]
        kept.append(
            (flat_in, first_norm, query, key, value, logsums, flat_heads, middle, second_norm, upper, active, up_grad)
        )

    def both(left, right):
        return sum(
            jnp.einsum("rd,rf->df", a, b, preferred_element_type=F32) for a, b in zip(left, right)
        )

    lows = [k[11].astype(BF) for k in kept]
    lower_grad = scatter_rows(both(lows, [k[10] for k in kept]), hidden // 2)
    upper_grads, seconds = [], []
    for micro in range(micro_count):
        upper = kept[micro][9]
        active_grad = jnp.dot(lows[micro], lower_t, preferred_element_type=F32)
        upper_grad = jax.vjp(gelu_exact, upper)[1](active_grad)[0].astype(BF)
        upper_grads.append(upper_grad)
        seconds.append(
            jnp.einsum("rf,df->rd", upper_grad, upper_c, preferred_element_type=F32).astype(BF)
        )
    upper_wgrad = scatter_rows(both([k[8] for k in kept], upper_grads), hidden // 2)
    middle_grads, attn_lows, mixed_grads, gain_two_grad = [], [], [], 0.0
    for micro in range(micro_count):
        flat_in, first_norm, query, key, value, logsums, flat_heads, middle, _, _, _, up_grad = kept[micro]
        second_back = sum_pair(seconds[micro])
        middle_part, gain_part = jax.vjp(scaled_norm, middle, gain_two)[1](second_back)
        gain_two_grad = gain_two_grad + gain_part
        middle_grad = up_grad + middle_part
        attn_low = middle_grad.astype(BF)
        head_grads = jnp.dot(attn_low, output_t, preferred_element_type=F32).astype(BF)
        head_grads = head_grads.reshape(row_count, head_count, HD)
        query_grads, key_grads, value_grads = attend_backward(
            query, key, value, head_grads, logsums, lengths[micro, 0]
        )
        mixed_grad = jnp.stack(
            [rotate(query_grads, cosine, -sine), rotate(key_grads, cosine, -sine), value_grads],
            axis=1,
        )
        mixed_grads.append(mixed_grad.astype(BF).reshape(-1, proj_cols))
        middle_grads.append(middle_grad)
        attn_lows.append(attn_low)
    output_part = both(attn_lows, [k[6] for k in kept])
    proj_part = both([k[1] for k in kept], mixed_grads)
    one_grad = scatter_rows(
        jnp.concatenate([proj_part, output_part], axis=1), (proj_cols + feat_count) // 2
    )
    gain_one_grad, input_grads = 0.0, []
    for micro in range(micro_count):
        flat_in, _, _, _, _, _, _, middle, _, _, active, _ = kept[micro]
        ffn_part = jnp.einsum("rf,df->rd", active, lower_t, preferred_element_type=F32)
        result = middle + sum_pair(ffn_part.astype(BF))
        results_list.append(result.astype(BF).reshape(inputs.shape[1:]))
        first_back = jnp.einsum(
            "rc,dc->rd", mixed_grads[micro], proj_c, preferred_element_type=F32
        ).astype(BF)
        input_part, gain_part = jax.vjp(scaled_norm, flat_in, gain_one)[1](sum_pair(first_back))
        gain_one_grad = gain_one_grad + gain_part
        input_grads.append((middle_grads[micro] + input_part).reshape(inputs.shape[1:]))
    gain_parts = jnp.stack([gain_one_grad, gain_two_grad]).reshape(2, -1, shard_rows)
    gain_parts = lax.all_to_all(gain_parts.transpose(1, 0, 2), "dp", 0, 0, tiled=True)
    gains_grad = jnp.sum(gain_parts, axis=0)
    proj_grad = one_grad[:, :proj_cols].reshape(proj_weight.shape)
    output_grad = one_grad[:, proj_cols:].T
    lower_grad = lower_grad.T

    updates = [
        adamw_update(proj_weight, proj_first, proj_second, proj_grad, RATE_MATRIX, DECAY),
        adamw_update(output_weight, output_first, output_second, output_grad, RATE_OUTPUT, DECAY),
        adamw_update(upper_weight, upper_first, upper_second, upper_wgrad, RATE_MATRIX, DECAY),
        adamw_update(lower_weight, lower_first, lower_second, lower_grad, RATE_MATRIX, DECAY),
        adamw_update(norm_gains, gains_first, gains_second, gains_grad, RATE_GAIN, 0.0),
    ]
    return (
        jnp.stack(results_list),
        jnp.stack(input_grads),
        *[u[0] for u in updates],
        *[u[1] for u in updates],
        *[u[2] for u in updates],
        *[u[0].astype(BF) for u in updates],
    )


def solution(mesh):
    rows = P(None, "dp", None, None)
    weights = (P("dp", None, "mp"), P("mp", "dp"), P("dp", "mp"), P("mp", "dp"), P(None, "dp"))
    in_specs = (rows, rows, P(None, "dp"), *weights * 3)
    out_specs = (rows, rows, *weights * 4)
    return jax.shard_map(shards, mesh=mesh, in_specs=in_specs, out_specs=out_specs, check_vma=False)
```

time: 1140 us -> 395 us (0.35)
  waiting for transfers between devices: 829 us -> 107 us
  blocking collectives: 81.8 us -> 0 us
  starting transfers between devices: 1.62 us -> 82.7 us
  matrix products: 105 us -> 73.3 us
  local copies, waits for them, and re-layouts: 34.6 us -> 48.1 us
  between operations: 16 us -> 3.28 us
    reduce_scatter x4 -> x0, waiting for transfers between devices: 524 us -> none  [the longest x1 140 us: shards(): lax.psum_scatter(grads[2], 'dp', scatter_dimension=0, tiled=True)]
    all_gather x3 -> x0, waiting for transfers between devices: 127 us -> none  [the longest x1 64.3 us: shards(): lax.all_gather(upper_weight.astype(jnp.bfloat16), 'dp', axis=0, tiled=True)]
    unnamed x13 -> x0, waiting for transfers between devices: 116 us -> none
    ppermute x0 -> x50, waiting for transfers between devices: none -> 105 us  [the longest x42 105 us: exchange(): return lax.ppermute(value, 'dp', pairs)]
    all_gather x2 -> x0, blocking collectives: 81.8 us -> none  [the longest x1 42.2 us: shards(): lax.all_gather(norm_gains.astype(jnp.bfloat16), 'dp', axis=1, tiled=True)]
    ppermute x0 -> x50, starting transfers between devices: none -> 73.6 us  [the longest x42 72.2 us: exchange(): return lax.ppermute(value, 'dp', pairs)]
    psum x4 -> x0, waiting for transfers between devices: 62.1 us -> none  [the longest x2 35.1 us: shards(): lax.psum(attn_part.astype(jnp.bfloat16), 'mp').astype(jnp.float32)]
    dot_general x36, matrix products: 105 us -> 73.3 us  [the longest x2 18.5 us: shards(): upper = jnp.dot(second_norm, upper_c, preferred_element_type=F32)]
  transfers between devices with their start and end apart: 12 -> 51, of which waited for: 11 -> 25; matrix products, arithmetic and copies ran while one was open for 5% -> 26% of each run, Pallas kernels for 0% -> 0%
where the time goes in v1:
time: 395 us; the launch traced here: 388 us
  waiting for transfers between devices  107 us (27%)
  starting transfers between devices  82.7 us (21%)
  other arithmetic  73.9 us (19%)
  matrix products  73.3 us (19%)
  local copies, waits for them, and re-layouts  48.1 us (12%)
    ppermute x42, waiting for transfers between devices, exchange(): return lax.ppermute(value, 'dp', pairs)  105 us
    ppermute x42, starting transfers between devices, exchange(): return lax.ppermute(value, 'dp', pairs)  72.2 us
    unnamed x263, local copies, waits for them, and re-layouts  21.8 us
    dot_general x2, matrix products, shards(): upper = jnp.dot(second_norm, upper_c, preferred_element_type=F32)  18.5 us
    gather x3, local copies, waits for them, and re-layouts, gather_rows(): whole = jnp.take(whole, order, axis=2).transpose(2, 0, 1, 3, 4)  11.7 us
    dot_general x8, matrix products, both(): jnp.einsum('rd,rf->df', a, b, preferred_element_type=F32)  10.5 us
    all_to_all x1, starting transfers between devices, shards(): lax.all_to_all(gain_parts.transpose(1, 0, 2), 'dp', 0, 0, tiled=True)  9.17 us
  transfers between devices with their start and end apart: 51, of which 25 were waited for; matrix products, arithmetic and copies ran while one was open for 26% of the time, Pallas kernels for 0%

profile of v1, /device:TPU:0, one launch (start us, length us, event | category | flops | bytes accessed | tf_op | source)
XLA Modules:
  0.0 388.3 jit_solution(5988362720720935509)
XLA Ops:
  1.8 4.1 %collective-permute-start.9 = (bf16[48,1536]{1,0:T(8,128)(2,1)S(1)}, bf16[48,1536]{1,0:T(8,128)(2,1)S(1)}, u32[]{:S(2)}, u32[]{:S(2)}) collective-permute-start(bf16[48,1536]{1,0:T(8,128)(2,1)S(1)} %convert_element_type.658), channel_id=1, source_target_pairs={{0,16},{2,18},{4,20},{6,22},{8,24},{10,26},{12,28},{14,30},{16,0},... | collective-permute-start | bytes 442376 | tf_op jit(solution)/shard_map/ppermute | solution.py:50
  36.3 7.9 %collective-permute-done.3 = bf16[4,48,896]{2,1,0:T(8,128)(2,1)S(1)} collective-permute-done((bf16[4,48,896]{2,1,0:T(8,128)(2,1)S(1)}, bf16[4,48,896]{2,1,0:T(8,128)(2,1)S(1)}, u32[]{:S(2)}, u32[]{:S(2)}) %collective-permute-start.3) | collective-permute-done | bytes 344096 | tf_op jit(solution)/shard_map/ppermute | solution.py:50
  46.9 6.9 %collective-permute-done.12 = bf16[2,4,48,768]{3,2,1,0:T(8,128)(2,1)S(1)} collective-permute-done((bf16[2,4,48,768]{3,2,1,0:T(8,128)(2,1)S(1)}, bf16[2,4,48,768]{3,2,1,0:T(8,128)(2,1)S(1)}, u32[]{:S(2)}, u32[]{:S(2)}) %collective-permute-start.12) | collective-permute-done | bytes 589856 | tf_op jit(solution)/shard_map/ppermute | solution.py:50
  58.0 7.8 %collective-permute-done.4 = bf16[2,4,48,896]{3,2,1,0:T(8,128)(2,1)S(1)} collective-permute-done((bf16[2,4,48,896]{3,2,1,0:T(8,128)(2,1)S(1)}, bf16[2,4,48,896]{3,2,1,0:T(8,128)(2,1)S(1)}, u32[]{:S(2)}, u32[]{:S(2)}) %collective-permute-start.4) | collective-permute-done | bytes 688160 | tf_op jit(solution)/shard_map/ppermute | solution.py:50
  67.7 4.0 %gather_fusion = bf16[4,2,2,48,1664]{4,3,2,1,0:T(8,128)(2,1)} fusion(bf16[2,2,4,48,1664]{4,3,2,1,0:T(8,128)(2,1)} %pad_maximum_fusion.2, s32[1024]{0:T(1024)S(1)} %pad_clamp_fusion.1), kind=kCustom, calls=%fused_computation.2 | custom fusion | bytes 5111824 | tf_op jit(solution)/shard_map/jit(_take)/gather | solution.py:71
  112.3 9.2 %multiply_convert_fusion.3 = (bf16[512,1536]{1,0:T(8,128)(2,1)S(1)}, f32[512,1536]{1,0:T(8,128)}, f32[512,1536]{1,0:T(8,128)}) fusion(bf16[768,1536]{1,0:T(8,128)(2,1)S(1)} %bitcast.507, f32[512,768]{1,0:T(8,128)S(1)} %get-tuple-element.134, f32[768]{0:T(1024)S(1)} %get-tuple-element.105, f32[512]{0:T(512)S(1)} %fusion.207, f32[512]{0:T(512)S(1)} %broadcast_multiply_fusion.2), kind=kOutput, calls=%fused_computation.47 | convolution fusion | flops 1260650496 | bytes 11803648 | tf_op jit(solution)/shard_map/dot_general | solution.py:257
  121.6 9.2 %multiply_convert_fusion.2 = (bf16[512,1536]{1,0:T(8,128)(2,1)S(1)}, f32[512,1536]{1,0:T(8,128)}, f32[512,1536]{1,0:T(8,128)}) fusion(bf16[768,1536]{1,0:T(8,128)(2,1)S(1)} %bitcast.508, f32[512,768]{1,0:T(8,128)S(1)} %get-tuple-element.154, f32[512]{0:T(512)S(1)} %fusion.209, f32[512]{0:T(512)S(1)} %broadcast_multiply_fusion, f32[768]{0:T(1024)S(1)} %get-tuple-element.105), kind=kOutput, calls=%fused_computation.34 | convolution fusion | flops 1260650496 | bytes 11803648 | tf_op jit(solution)/shard_map/dot_general | solution.py:257
  143.6 10.4 %collective-permute-done.43 = bf16[4,2,48,768]{3,2,0,1:T(8,128)(2,1)} collective-permute-done((bf16[4,2,48,768]{3,2,0,1:T(8,128)(2,1)}, bf16[4,2,48,768]{3,2,0,1:T(8,128)(2,1)}, u32[]{:S(2)}, u32[]{:S(2)}) %collective-permute-start.43) | collective-permute-done | bytes 589856 | tf_op jit(solution)/shard_map/ppermute | solution.py:50
  169.8 4.4 %collective-permute-start.47 = (bf16[48,1536]{1,0:T(8,128)(2,1)}, bf16[48,1536]{1,0:T(8,128)(2,1)}, u32[]{:S(2)}, u32[]{:S(2)}) collective-permute-start(bf16[48,1536]{1,0:T(8,128)(2,1)} %get-tuple-element.155), channel_id=1, source_target_pairs={{0,8},{2,10},{4,12},{6,14},{8,16},{10,18},{12,20},{14,22},{16,24},... | collective-permute-start | bytes 442376 | tf_op jit(solution)/shard_map/ppermute | solution.py:50
  179.1 5.0 %collective-permute-done.48 = bf16[48,1536]{1,0:T(8,128)(2,1)} collective-permute-done((bf16[48,1536]{1,0:T(8,128)(2,1)}, bf16[48,1536]{1,0:T(8,128)(2,1)}, u32[]{:S(2)}, u32[]{:S(2)}) %collective-permute-start.48) | collective-permute-done | bytes 147488 | tf_op jit(solution)/shard_map/ppermute | solution.py:50
  194.7 6.1 %collective-permute-done.16 = bf16[48,1536]{1,0:T(8,128)(2,1)S(1)} collective-permute-done((bf16[48,1536]{1,0:T(8,128)(2,1)S(1)}, bf16[48,1536]{1,0:T(8,128)(2,1)S(1)}, u32[]{:S(2)}, u32[]{:S(2)}) %collective-permute-start.16) | collective-permute-done | bytes 147488 | tf_op jit(solution)/shard_map/ppermute | solution.py:50
  203.8 5.2 %collective-permute-done.18 = bf16[4,48,768]{2,1,0:T(8,128)(2,1)S(1)} collective-permute-done((bf16[4,48,768]{2,1,0:T(8,128)(2,1)S(1)}, bf16[4,48,768]{2,1,0:T(8,128)(2,1)S(1)}, u32[]{:S(2)}, u32[]{:S(2)}) %collective-permute-start.18) | collective-permute-done | bytes 294944 | tf_op jit(solution)/shard_map/ppermute | solution.py:50
  214.2 8.2 %collective-permute-done.19 = bf16[2,4,48,768]{3,2,1,0:T(8,128)(2,1)S(1)} collective-permute-done((bf16[2,4,48,768]{3,2,1,0:T(8,128)(2,1)S(1)}, bf16[2,4,48,768]{3,2,1,0:T(8,128)(2,1)S(1)}, u32[]{:S(2)}, u32[]{:S(2)}) %collective-permute-start.19) | collective-permute-done | bytes 589856 | tf_op jit(solution)/shard_map/ppermute | solution.py:50
  225.0 4.0 %gather_fusion.2 = bf16[4,2,2,48,1536]{4,3,1,2,0:T(8,128)(2,1)} fusion(bf16[2,2,4,48,1536]{4,3,2,0,1:T(8,128)(2,1)} %pad_maximum_fusion.4, s32[1024]{0:T(1024)} %copy-done.116), kind=kCustom, calls=%fused_computation.1.clone | custom fusion | bytes 4718608 | tf_op jit(solution)/shard_map/jit(_take)/gather | solution.py:71
  252.1 5.4 %collective-permute-done.36 = bf16[4,2,48,768]{3,2,0,1:T(8,128)(2,1)S(1)} collective-permute-done((bf16[4,2,48,768]{3,2,0,1:T(8,128)(2,1)S(1)}, bf16[4,2,48,768]{3,2,0,1:T(8,128)(2,1)S(1)}, u32[]{:S(2)}, u32[]{:S(2)}) %collective-permute-start.36) | collective-permute-done | bytes 589856 | tf_op jit(solution)/shard_map/ppermute | solution.py:50
  258.5 5.5 %collective-permute-done.38 = bf16[4,2,48,768]{3,2,0,1:T(8,128)(2,1)S(1)} collective-permute-done((bf16[4,2,48,768]{3,2,0,1:T(8,128)(2,1)S(1)}, bf16[4,2,48,768]{3,2,0,1:T(8,128)(2,1)S(1)}, u32[]{:S(2)}, u32[]{:S(2)}) %collective-permute-start.38) | collective-permute-done | bytes 589856 | tf_op jit(solution)/shard_map/ppermute | solution.py:50
  277.6 5.3 %multiply_reduce_fusion = (f32[6,512]{1,0:T(8,128)S(1)}, f32[6,512,512]{1,2,0:T(8,128)}) fusion(f32[6,512,512]{1,2,0:T(8,128)S(1)} %bitcast.481, f32[6,512]{1,0:T(8,128)S(1)} %copy-done.85, bf16[512,6,64]{0,2,1:T(8,128)(2,1)S(1)} %bitcast.522, f32[512,3,6,64]{0,3,2,1:T(8,128)} %copy-done.49), kind=kOutput, calls=%fused_computation.4 | convolution fusion | flops 206042112 | bytes 13393920 | tf_op jit(solution)/shard_map/qhd,hkd->hqk/dot_general | solution.py:171
  282.9 4.7 %multiply_convert_fusion = bf16[6,512,512]{1,2,0:T(8,128)(2,1)S(1)} fusion(f32[6,512,512]{1,2,0:T(8,128)} %get-tuple-element.230, f32[6,512,512]{1,2,0:T(8,128)S(1)} %bitcast.481, f32[6,512]{1,0:T(8,128)S(1)} %get-tuple-element.229, f32[6,512]{1,0:T(8,128)S(1)} %copy-done.85), kind=kLoop, calls=%fused_computation.3 | loop fusion | flops 6291456 | bytes 15753216 | tf_op jit(solution)/shard_map/convert_element_type | solution.py:173
  317.7 4.0 %collective-permute-start.40 = (bf16[48,1536]{1,0:T(8,128)(2,1)S(1)}, bf16[48,1536]{1,0:T(8,128)(2,1)S(1)}, u32[]{:S(2)}, u32[]{:S(2)}) collective-permute-start(bf16[48,1536]{1,0:T(8,128)(2,1)S(1)} %get-tuple-element.158), channel_id=1, source_target_pairs={{0,8},{2,10},{4,12},{6,14},{8,16},{10,18},{12,20},{14,22},{16,24},... | collective-permute-start | bytes 442376 | tf_op jit(solution)/shard_map/ppermute | solution.py:50
  327.0 5.4 %collective-permute-done.41 = bf16[48,1536]{1,0:T(8,128)(2,1)S(1)} collective-permute-done((bf16[48,1536]{1,0:T(8,128)(2,1)S(1)}, bf16[48,1536]{1,0:T(8,128)(2,1)S(1)}, u32[]{:S(2)}, u32[]{:S(2)}) %collective-permute-start.41) | collective-permute-done | bytes 147488 | tf_op jit(solution)/shard_map/ppermute | solution.py:50
  335.1 5.3 %collective-permute-done.29 = bf16[4,2,48,768]{3,2,0,1:T(8,128)(2,1)S(1)} collective-permute-done((bf16[4,2,48,768]{3,2,0,1:T(8,128)(2,1)S(1)}, bf16[4,2,48,768]{3,2,0,1:T(8,128)(2,1)S(1)}, u32[]{:S(2)}, u32[]{:S(2)}) %collective-permute-start.29) | collective-permute-done | bytes 589856 | tf_op jit(solution)/shard_map/ppermute | solution.py:50
  342.1 6.6 %collective-permute-done.31 = bf16[4,2,48,768]{3,2,0,1:T(8,128)(2,1)S(1)} collective-permute-done((bf16[4,2,48,768]{3,2,0,1:T(8,128)(2,1)S(1)}, bf16[4,2,48,768]{3,2,0,1:T(8,128)(2,1)S(1)}, u32[]{:S(2)}, u32[]{:S(2)}) %collective-permute-start.31) | collective-permute-done | bytes 589856 | tf_op jit(solution)/shard_map/ppermute | solution.py:50
  356.2 9.2 %all-to-all-start = ((f32[16,2,48]{2,1,0:T(2,128)}), f32[16,2,48]{2,1,0:T(2,128)S(1)}, u32[]{:S(2)}, u32[]{:S(2)}) async-start(f32[16,2,48]{2,1,0:T(2,128)} %maximum_bitcast_fusion.20), calls=%async_computation | async-start | bytes 32768 | tf_op jit(solution)/shard_map/all_to_all | solution.py:320
  382.1 4.1 %collective-permute-done.34 = bf16[48,1536]{1,0:T(8,128)(2,1)S(1)} collective-permute-done((bf16[48,1536]{1,0:T(8,128)(2,1)S(1)}, bf16[48,1536]{1,0:T(8,128)(2,1)S(1)}, u32[]{:S(2)}, u32[]{:S(2)}) %collective-permute-start.34) | collective-permute-done | bytes 147488 | tf_op jit(solution)/shard_map/ppermute | solution.py:50
  (528 shorter events, 236.8 us)
Async XLA Ops:
  1.8 19.3 %collective-permute-start.9 = (bf16[48,1536]{1,0:T(8,128)(2,1)S(1)}, bf16[48,1536]{1,0:T(8,128)(2,1)S(1)}, u32[]{:S(2)}, u32[]{:S(2)}) collective-permute-start(bf16[48,1536]{1,0:T(8,128)(2,1)S(1)} %convert_element_type.658), channel_id=1, source_target_pairs={{0,16},{2,18},{4,20},{6,22},{8,24},{10,26},{12,28},{14,30},{16,0},... | collective-permute-start | bytes 442376 | tf_op jit(solution)/shard_map/ppermute | solution.py:50
  5.9 18.6 %collective-permute-start.8 = (bf16[48,1536]{1,0:T(8,128)(2,1)S(1)}, bf16[48,1536]{1,0:T(8,128)(2,1)S(1)}, u32[]{:S(2)}, u32[]{:S(2)}) collective-permute-start(bf16[48,1536]{1,0:T(8,128)(2,1)S(1)} %convert_element_type.658), channel_id=1, source_target_pairs={{0,8},{2,10},{4,12},{6,14},{8,16},{10,18},{12,20},{14,22},{16,24},... | collective-permute-start | bytes 442376 | tf_op jit(solution)/shard_map/ppermute | solution.py:50
  7.5 17.0 %collective-permute-start.10 = (bf16[48,1536]{1,0:T(8,128)(2,1)S(1)}, bf16[48,1536]{1,0:T(8,128)(2,1)S(1)}, u32[]{:S(2)}, u32[]{:S(2)}) collective-permute-start(bf16[48,1536]{1,0:T(8,128)(2,1)S(1)} %convert_element_type.658), channel_id=1, source_target_pairs={{0,24},{2,26},{4,28},{6,30},{8,0},{10,2},{12,4},{14,6},{16,8},{18,... | collective-permute-start | bytes 442376 | tf_op jit(solution)/shard_map/ppermute | solution.py:50
  12.4 18.0 %collective-permute-start.1 = (bf16[48,1664]{1,0:T(8,128)(2,1)S(1)}, bf16[48,1664]{1,0:T(8,128)(2,1)S(1)}, u32[]{:S(2)}, u32[]{:S(2)}) collective-permute-start(bf16[48,1664]{1,0:T(8,128)(2,1)S(1)} %get-tuple-element.198), channel_id=1, source_target_pairs={{0,16},{2,18},{4,20},{6,22},{8,24},{10,26},{12,28},{14,30},{16,0},... | collective-permute-start | bytes 479240 | tf_op jit(solution)/shard_map/ppermute | solution.py:50
  12.5 17.9 %collective-permute-start = (bf16[48,1664]{1,0:T(8,128)(2,1)S(1)}, bf16[48,1664]{1,0:T(8,128)(2,1)S(1)}, u32[]{:S(2)}, u32[]{:S(2)}) collective-permute-start(bf16[48,1664]{1,0:T(8,128)(2,1)S(1)} %get-tuple-element.198), channel_id=1, source_target_pairs={{0,8},{2,10},{4,12},{6,14},{8,16},{10,18},{12,20},{14,22},{16,24},... | collective-permute-start | bytes 479240 | tf_op jit(solution)/shard_map/ppermute | solution.py:50
  34.8 19.0 %collective-permute-start.12 = (bf16[2,4,48,768]{3,2,1,0:T(8,128)(2,1)S(1)}, bf16[2,4,48,768]{3,2,1,0:T(8,128)(2,1)S(1)}, u32[]{:S(2)}, u32[]{:S(2)}) collective-permute-start(bf16[2,4,48,768]{3,2,1,0:T(8,128)(2,1)S(1)} %maximum_select_fusion.10), channel_id=1, source_target_pairs={{0,4},{2,6},{4,0},{6,2},{8,12},{10,14},{12,8},{14,10},{16,20},{18,... | collective-permute-start | bytes 1769480 | tf_op jit(solution)/shard_map/ppermute | solution.py:50
  35.5 21.3 %collective-permute-start.14 = (bf16[2,4,48,768]{3,2,1,0:T(8,128)(2,1)S(1)}, bf16[2,4,48,768]{3,2,1,0:T(8,128)(2,1)S(1)}, u32[]{:S(2)}, u32[]{:S(2)}) collective-permute-start(bf16[2,4,48,768]{3,2,1,0:T(8,128)(2,1)S(1)} %maximum_select_fusion.12), channel_id=1, source_target_pairs={{0,2},{2,0},{4,6},{6,4},{8,10},{10,8},{12,14},{14,12},{16,18},{18,... | collective-permute-start | bytes 1769480 | tf_op jit(solution)/shard_map/ppermute | solution.py:50
  44.3 21.5 %collective-permute-start.4 = (bf16[2,4,48,896]{3,2,1,0:T(8,128)(2,1)S(1)}, bf16[2,4,48,896]{3,2,1,0:T(8,128)(2,1)S(1)}, u32[]{:S(2)}, u32[]{:S(2)}) collective-permute-start(bf16[2,4,48,896]{3,2,1,0:T(8,128)(2,1)S(1)} %maximum_select_fusion.7), channel_id=1, source_target_pairs={{0,4},{2,6},{4,0},{6,2},{8,12},{10,14},{12,8},{14,10},{16,20},{18,... | collective-permute-start | bytes 2064392 | tf_op jit(solution)/shard_map/ppermute | solution.py:50
  44.8 21.3 %collective-permute-start.6 = (bf16[2,4,48,768]{3,2,1,0:T(8,128)(2,1)S(1)}, bf16[2,4,48,768]{3,2,1,0:T(8,128)(2,1)S(1)}, u32[]{:S(2)}, u32[]{:S(2)}) collective-permute-start(bf16[2,4,48,768]{3,2,1,0:T(8,128)(2,1)S(1)} %maximum_select_fusion.9), channel_id=1, source_target_pairs={{0,2},{2,0},{4,6},{6,4},{8,10},{10,8},{12,14},{14,12},{16,18},{18,... | collective-permute-start | bytes 1769480 | tf_op jit(solution)/shard_map/ppermute | solution.py:50
  91.8 15.8 %collective-permute-start.7 = (bf16[512,768]{1,0:T(8,128)(2,1)S(1)}, bf16[512,768]{1,0:T(8,128)(2,1)}, u32[]{:S(2)}, u32[]{:S(2)}) collective-permute-start(bf16[512,768]{1,0:T(8,128)(2,1)S(1)} %convolution_convert_fusion.7), channel_id=1, source_target_pairs={{0,1},{1,0},{2,3},{3,2},{4,5},{5,4},{6,7},{7,6},{8,9},{9,8},{10,11... | collective-permute-start | bytes 2359304 | tf_op jit(solution)/shard_map/ppermute | solution.py:105
  138.4 15.6 %collective-permute-start.43 = (bf16[4,2,48,768]{3,2,0,1:T(8,128)(2,1)}, bf16[4,2,48,768]{3,2,0,1:T(8,128)(2,1)}, u32[]{:S(2)}, u32[]{:S(2)}) collective-permute-start(bf16[4,2,48,768]{3,2,0,1:T(8,128)(2,1)} %fusion.115), channel_id=1, source_target_pairs={{0,2},{2,0},{4,6},{6,4},{8,10},{10,8},{12,14},{14,12},{16,18},{18,... | collective-permute-start | bytes 1769480 | tf_op jit(solution)/shard_map/ppermute | solution.py:50
  142.1 15.3 %collective-permute-start.45 = (bf16[4,2,48,768]{3,2,0,1:T(8,128)(2,1)}, bf16[4,2,48,768]{3,2,0,1:T(8,128)(2,1)}, u32[]{:S(2)}, u32[]{:S(2)}) collective-permute-start(bf16[4,2,48,768]{3,2,0,1:T(8,128)(2,1)} %fusion.116), channel_id=1, source_target_pairs={{0,4},{2,6},{4,0},{6,2},{8,12},{10,14},{12,8},{14,10},{16,20},{18,... | collective-permute-start | bytes 1769480 | tf_op jit(solution)/shard_map/ppermute | solution.py:50
  247.9 18.8 %collective-permute-start.27 = (bf16[512,768]{1,0:T(8,128)(2,1)S(1)}, bf16[512,768]{1,0:T(8,128)(2,1)S(1)}, u32[]{:S(2)}, u32[]{:S(2)}) collective-permute-start(bf16[512,768]{1,0:T(8,128)(2,1)S(1)} %convolution_convert_fusion), channel_id=1, source_target_pairs={{0,1},{1,0},{2,3},{3,2},{4,5},{5,4},{6,7},{7,6},{8,9},{9,8},{10,11... | collective-permute-start | bytes 2359304 | tf_op jit(solution)/shard_map/ppermute | solution.py:105
  248.0 19.0 %collective-permute-start.25 = (bf16[512,768]{1,0:T(8,128)(2,1)S(1)}, bf16[512,768]{1,0:T(8,128)(2,1)S(1)}, u32[]{:S(2)}, u32[]{:S(2)}) collective-permute-start(bf16[512,768]{1,0:T(8,128)(2,1)S(1)} %convolution_convert_fusion.1), channel_id=1, source_target_pairs={{0,1},{1,0},{2,3},{3,2},{4,5},{5,4},{6,7},{7,6},{8,9},{9,8},{10,11... | collective-permute-start | bytes 2359304 | tf_op jit(solution)/shard_map/ppermute | solution.py:105
  248.5 15.5 %collective-permute-start.38 = (bf16[4,2,48,768]{3,2,0,1:T(8,128)(2,1)S(1)}, bf16[4,2,48,768]{3,2,0,1:T(8,128)(2,1)S(1)}, u32[]{:S(2)}, u32[]{:S(2)}) collective-permute-start(bf16[4,2,48,768]{3,2,0,1:T(8,128)(2,1)S(1)} %fusion.114), channel_id=1, source_target_pairs={{0,4},{2,6},{4,0},{6,2},{8,12},{10,14},{12,8},{14,10},{16,20},{18,... | collective-permute-start | bytes 1769480 | tf_op jit(solution)/shard_map/ppermute | solution.py:50
  252.0 16.8 %collective-permute-start.22 = (bf16[512,768]{1,0:T(8,128)(2,1)S(1)}, bf16[512,768]{1,0:T(8,128)(2,1)S(1)}, u32[]{:S(2)}, u32[]{:S(2)}) collective-permute-start(bf16[512,768]{1,0:T(8,128)(2,1)S(1)} %convolution_convert_fusion.3), channel_id=1, source_target_pairs={{0,1},{1,0},{2,3},{3,2},{4,5},{5,4},{6,7},{7,6},{8,9},{9,8},{10,11... | collective-permute-start | bytes 2359304 | tf_op jit(solution)/shard_map/ppermute | solution.py:105
  264.0 51.0 %collective-permute-start.37 = (bf16[4,48,768]{2,1,0:T(8,128)(2,1)}, bf16[4,48,768]{2,1,0:T(8,128)(2,1)}, u32[]{:S(2)}, u32[]{:S(2)}) collective-permute-start(bf16[4,48,768]{2,1,0:T(8,128)(2,1)} %fusion.134), channel_id=1, source_target_pairs={{0,4},{2,6},{4,0},{6,2},{8,12},{10,14},{12,8},{14,10},{16,20},{18,... | collective-permute-start | bytes 884744 | tf_op jit(solution)/shard_map/ppermute | solution.py:50
  266.7 49.7 %collective-permute-start.39 = (bf16[4,48,768]{2,1,0:T(8,128)(2,1)}, bf16[4,48,768]{2,1,0:T(8,128)(2,1)}, u32[]{:S(2)}, u32[]{:S(2)}) collective-permute-start(bf16[4,48,768]{2,1,0:T(8,128)(2,1)} %fusion.135), channel_id=1, source_target_pairs={{0,2},{2,0},{4,6},{6,4},{8,10},{10,8},{12,14},{14,12},{16,18},{18,... | collective-permute-start | bytes 884744 | tf_op jit(solution)/shard_map/ppermute | solution.py:50
  314.9 36.2 %collective-permute-start.28 = (bf16[512,768]{1,0:T(8,128)(2,1)S(1)}, bf16[512,768]{1,0:T(8,128)(2,1)S(1)}, u32[]{:S(2)}, u32[]{:S(2)}) collective-permute-start(bf16[512,768]{1,0:T(8,128)(2,1)S(1)} %convolution_convert_fusion.4), channel_id=1, source_target_pairs={{0,1},{1,0},{2,3},{3,2},{4,5},{5,4},{6,7},{7,6},{8,9},{9,8},{10,11... | collective-permute-start | bytes 2359304 | tf_op jit(solution)/shard_map/ppermute | solution.py:105
  326.9 24.2 %collective-permute-start.26 = (bf16[512,768]{1,0:T(8,128)(2,1)S(1)}, bf16[512,768]{1,0:T(8,128)(2,1)S(1)}, u32[]{:S(2)}, u32[]{:S(2)}) collective-permute-start(bf16[512,768]{1,0:T(8,128)(2,1)S(1)} %convolution_convert_fusion.5), channel_id=1, source_target_pairs={{0,1},{1,0},{2,3},{3,2},{4,5},{5,4},{6,7},{7,6},{8,9},{9,8},{10,11... | collective-permute-start | bytes 2359304 | tf_op jit(solution)/shard_map/ppermute | solution.py:105
  332.5 16.3 %collective-permute-start.31 = (bf16[4,2,48,768]{3,2,0,1:T(8,128)(2,1)S(1)}, bf16[4,2,48,768]{3,2,0,1:T(8,128)(2,1)S(1)}, u32[]{:S(2)}, u32[]{:S(2)}) collective-permute-start(bf16[4,2,48,768]{3,2,0,1:T(8,128)(2,1)S(1)} %fusion.112), channel_id=1, source_target_pairs={{0,4},{2,6},{4,0},{6,2},{8,12},{10,14},{12,8},{14,10},{16,20},{18,... | collective-permute-start | bytes 1769480 | tf_op jit(solution)/shard_map/ppermute | solution.py:50
  340.6 32.1 %collective-permute-start.30 = (bf16[4,48,768]{2,1,0:T(8,128)(2,1)S(1)}, bf16[4,48,768]{2,1,0:T(8,128)(2,1)}, u32[]{:S(2)}, u32[]{:S(2)}) collective-permute-start(bf16[4,48,768]{2,1,0:T(8,128)(2,1)S(1)} %fusion.132), channel_id=1, source_target_pairs={{0,4},{2,6},{4,0},{6,2},{8,12},{10,14},{12,8},{14,10},{16,20},{18,... | collective-permute-start | bytes 884744 | tf_op jit(solution)/shard_map/ppermute | solution.py:50
  349.7 24.1 %collective-permute-start.32 = (bf16[4,48,768]{2,1,0:T(8,128)(2,1)}, bf16[4,48,768]{2,1,0:T(8,128)(2,1)}, u32[]{:S(2)}, u32[]{:S(2)}) collective-permute-start(bf16[4,48,768]{2,1,0:T(8,128)(2,1)} %fusion.133), channel_id=1, source_target_pairs={{0,2},{2,0},{4,6},{6,4},{8,10},{10,8},{12,14},{14,12},{16,18},{18,... | collective-permute-start | bytes 884744 | tf_op jit(solution)/shard_map/ppermute | solution.py:50
  356.2 16.5 %all-to-all-start = ((f32[16,2,48]{2,1,0:T(2,128)}), f32[16,2,48]{2,1,0:T(2,128)S(1)}, u32[]{:S(2)}, u32[]{:S(2)}) async-start(f32[16,2,48]{2,1,0:T(2,128)} %maximum_bitcast_fusion.20), calls=%async_computation | async-start | bytes 32768 | tf_op jit(solution)/shard_map/all_to_all | solution.py:320
  (157 other events, 1960.3 us)
